TPU v7x, 512 devices: a whole 4x4x16 slice. The times are simulated.
512 devices in a mesh: gossip: 16 (over x, z_lo), fsdp: 32 (over z_hi, y, core).
Axes of the slice: x: 4, y: 4, z: 16 (z_hi: 4, z_lo: 4; z = z_hi * 4 + z_lo), core: 2. Of those that a mesh axis runs over, the one named last changes fastest.
Arguments:
- activations: bfloat16 [16, 6144, 8192], P('gossip', 'fsdp'), may hold values from -6 to 6
- cotangent: bfloat16 [16, 6144, 256], P('gossip', 'fsdp'), may hold values from -0.3125 to 0.3125
- weights: bfloat16 [16, 8192, 256], P('gossip', 'fsdp'), may hold values from -0.0625 to 0.0625
- first_moment: float32 [16, 8192, 256], P('gossip', 'fsdp'), may hold values from -6 to 6
- second_moment: float32 [16, 8192, 256], P('gossip', 'fsdp'), may hold values from 0.1 to 10
- step_number: int32 [1], replicated, may hold values from 0 to 23
Outputs:
- keys_values: bfloat16 [16, 6144, 256], P('gossip', 'fsdp')
- new_weights: bfloat16 [16, 8192, 256], P('gossip', 'fsdp')
- new_first: float32 [16, 8192, 256], P('gossip', 'fsdp')
- new_second: float32 [16, 8192, 256], P('gossip', 'fsdp')
All inputs are finite; a program needn't handle non-finite values.
Results may differ from a plain program's by a relative error of at most 0.0045.
The roundings to bfloat16 on the way count: a program that leaves them out, or rounds other values in their place, can miss the bound.
Values may be sent and summed in bfloat16 or wider, within the bound.
A program may use at most 64 MiB of HBM per device.

v0:
```python
import jax
import jax.numpy as jnp
from jax import lax
from jax.sharding import PartitionSpec as P

beta_one = 0.9
beta_two = 0.95
learn_rate = 0.001
epsilon = 1e-08


def shifted(value, axis, steps):
    count = lax.axis_size(axis)
    pairs = [(source, (source + steps) % count) for source in range(count)]
    return lax.ppermute(value, axis, pairs)


def body(activations, cotangent, weights, first_moment, second_moment, step_number):
    inputs = activations[0]
    upstream = cotangent[0]
    shard = weights[0]
    columns = inputs
    projected = jnp.dot(
        columns,
        lax.all_gather(weights, "fsdp", axis=1, tiled=True)[0],
        preferred_element_type=jnp.float32,
    )
    columns = inputs
    gradient = lax.psum_scatter(
        lax.dot_general(
            columns, upstream, (((0,), (0,)), ((), ())), preferred_element_type=jnp.float32
        ).astype(jnp.bfloat16),
        "fsdp",
        scatter_dimension=0,
        tiled=True,
    ).astype(jnp.float32)
    counter = (step_number[0] + 1).astype(jnp.float32)
    correct_one = 1.0 - jnp.power(jnp.float32(beta_one), counter)
    correct_two = 1.0 - jnp.power(jnp.float32(beta_two), counter)
    next_one = beta_one * first_moment[0] + (1.0 - beta_one) * gradient
    next_two = beta_two * second_moment[0] + (1.0 - beta_two) * gradient * gradient
    update = next_one / correct_one / (jnp.sqrt(next_two / correct_two) + epsilon)
    local = (shard.astype(jnp.float32) - learn_rate * update).astype(jnp.bfloat16)
    distance = jnp.left_shift(jnp.int32(1), step_number[0] % 3)

    def one_hop(index, values):
        return shifted(values, "gossip", 1)

    partner = lax.fori_loop(0, distance, one_hop, local)
    mixed = ((local.astype(jnp.float32) + partner.astype(jnp.float32)) * 0.5).astype(jnp.bfloat16)
    return (projected.astype(jnp.bfloat16)[None], mixed[None], next_one[None], next_two[None])


def solution(mesh):
    placed = (
        P("gossip", "fsdp", None),
        P("gossip", "fsdp", None),
        P("gossip", "fsdp", None),
        P("gossip", "fsdp", None),
        P("gossip", "fsdp", None),
        P(),
    )
    return jax.shard_map(
        body,
        mesh=mesh,
        in_specs=placed,
        out_specs=(
            P("gossip", "fsdp", None),
            P("gossip", "fsdp", None),
            P("gossip", "fsdp", None),
            P("gossip", "fsdp", None),
        ),
        check_vma=False,
    )
```

profile of v0, /device:TPU:1, one launch (start us, length us, event | category | flops | bytes accessed | tf_op | source)
XLA Modules:
  0.0 264.5 jit_solution(1324228370037543317)
XLA Ops:
  7.2 0.0 copy-start
  7.2 0.0 reduce-scatter.2.cloned.1.call-start
  7.2 1.8 copy-done
  9.1 4.2 %convolution_convert_fusion = bf16[8192,256]{1,0:T(8,128)(2,1)} fusion(bf16[1,192,8192]{2,1,0:T(8,128)(2,1)S(1)} %copy-done, bf16[1,192,256]{2,1,0:T(8,128)(2,1)} %param.9), kind=kOutput, calls=%fused_computation | convolution fusion | flops 807403520 | bytes 7438336 | tf_op jit(solution)/shard_map/dot_general | solution.py:30
  13.3 0.0 copy-start.1
  13.3 0.0 reduce-scatter.2.cloned.1.call-update
  13.3 0.0 all-gather.2.cloned.1.call-start
  13.3 0.7 all-gather.2.cloned.1.call-update
  14.8 141.8 %reduce-scatter.2.cloned.1.call-done = bf16[256,256]{1,0:T(8,128)(2,1)} async-done(((bf16[8192,256]{1,0:T(8,128)(2,1)}), bf16[256,256]{1,0:T(8,128)(2,1)}) %reduce-scatter.2.cloned.1.call-update) | async-done | bytes 131088 | tf_op jit(solution)/shard_map/reduce_scatter | solution.py:29
  156.6 0.0 copy-done.1
  156.6 2.1 fusion.18
  158.7 40.2 %while.10 = (s32[]{:T(128)}, bf16[256,256]{1,0:T(8,128)(2,1)S(1)}, s32[]{:T(128)}, s32[]{:T(128)}) while((s32[]{:T(128)}, bf16[256,256]{1,0:T(8,128)(2,1)S(1)}, s32[]{:T(128)}, s32[]{:T(128)}) %tuple.24), condition=%wide.region_2.3_spmd, body=%wide.region_1.2_spmd.sunk | while | flops 2 | bytes 786525 | solution.py:49
  158.7 1.9 collective-permute-start
  160.7 7.7 %collective-permute-done = bf16[256,256]{1,0:T(8,128)(2,1)S(1)} collective-permute-done((bf16[256,256]{1,0:T(8,128)(2,1)S(1)}, bf16[256,256]{1,0:T(8,128)(2,1)S(1)}, u32[]{:S(2)}, u32[]{:S(2)}) %collective-permute-start) | collective-permute-done | bytes 131104 | tf_op jit(solution)/shard_map/while/body/ppermute | solution.py:15
  168.4 1.9 collective-permute-start
  170.3 7.7 %collective-permute-done = bf16[256,256]{1,0:T(8,128)(2,1)S(1)} collective-permute-done((bf16[256,256]{1,0:T(8,128)(2,1)S(1)}, bf16[256,256]{1,0:T(8,128)(2,1)S(1)}, u32[]{:S(2)}, u32[]{:S(2)}) %collective-permute-start) | collective-permute-done | bytes 131104 | tf_op jit(solution)/shard_map/while/body/ppermute | solution.py:15
  178.1 1.9 collective-permute-start
  180.0 8.3 %collective-permute-done = bf16[256,256]{1,0:T(8,128)(2,1)S(1)} collective-permute-done((bf16[256,256]{1,0:T(8,128)(2,1)S(1)}, bf16[256,256]{1,0:T(8,128)(2,1)S(1)}, u32[]{:S(2)}, u32[]{:S(2)}) %collective-permute-start) | collective-permute-done | bytes 131104 | tf_op jit(solution)/shard_map/while/body/ppermute | solution.py:15
  188.4 1.9 collective-permute-start
  190.3 8.6 %collective-permute-done = bf16[256,256]{1,0:T(8,128)(2,1)S(1)} collective-permute-done((bf16[256,256]{1,0:T(8,128)(2,1)S(1)}, bf16[256,256]{1,0:T(8,128)(2,1)S(1)}, u32[]{:S(2)}, u32[]{:S(2)}) %collective-permute-start) | collective-permute-done | bytes 131104 | tf_op jit(solution)/shard_map/while/body/ppermute | solution.py:15
  198.9 0.7 fusion.19
  199.6 54.2 %all-gather.2.cloned.1.call-done = bf16[1,8192,256]{2,1,0:T(8,128)(2,1)} async-done(((bf16[1,256,256]{2,1,0:T(8,128)(2,1)}), bf16[1,8192,256]{2,1,0:T(8,128)(2,1)}) %all-gather.2.cloned.1.call-update) | async-done | bytes 4194320 | tf_op jit(solution)/shard_map/all_gather | solution.py:25
  253.8 3.8 %fusion.9 = bf16[1,192,256]{2,1,0:T(8,128)(2,1)} fusion(bf16[1,8192,256]{2,1,0:T(8,128)(2,1)} %all-gather.2.cloned.1.call-done, bf16[1,192,8192]{2,1,0:T(8,128)(2,1)S(1)} %copy-done), kind=kOutput, calls=%fused_computation.6 | convolution fusion | flops 805355520 | bytes 7438336 | tf_op jit(solution)/shard_map/dot_general | solution.py:23
  (5 shorter events, 0.0 us)
Async XLA Ops:
  7.2 1.9 copy-start
  7.2 149.5 %reduce-scatter.2.cloned.1.call-start = ((), (), s32[]{:S(2)}) async-start(), calls=%async_computation.2 | async-start | bytes 4325376 | tf_op jit(solution)/shard_map/reduce_scatter | solution.py:29
  13.3 143.4 %copy-start.1 = (bf16[1,256,256]{2,1,0:T(8,128)(2,1)S(1)}, bf16[1,256,256]{2,1,0:T(8,128)(2,1)}, u32[]{:S(2)}) copy-start(bf16[1,256,256]{2,1,0:T(8,128)(2,1)} %param.10) | copy-start | bytes 393220
  13.3 240.5 %all-gather.2.cloned.1.call-start = ((), (), s32[]{:S(2)}) async-start(), calls=%async_computation.1 | async-start | bytes 4325376 | tf_op jit(solution)/shard_map/all_gather | solution.py:25
  158.7 9.6 %collective-permute-start = (bf16[256,256]{1,0:T(8,128)(2,1)S(1)}, bf16[256,256]{1,0:T(8,128)(2,1)S(1)}, u32[]{:S(2)}, u32[]{:S(2)}) collective-permute-start(bf16[256,256]{1,0:T(8,128)(2,1)S(1)} %get-tuple-element.57), channel_id=1, source_target_pairs={{0,32},{32,64},{64,96},{96,128},{128,160},{160,192},{192,224},{224... | collective-permute-start | bytes 393224 | tf_op jit(solution)/shard_map/while/body/ppermute | solution.py:15
  168.4 9.6 %collective-permute-start = (bf16[256,256]{1,0:T(8,128)(2,1)S(1)}, bf16[256,256]{1,0:T(8,128)(2,1)S(1)}, u32[]{:S(2)}, u32[]{:S(2)}) collective-permute-start(bf16[256,256]{1,0:T(8,128)(2,1)S(1)} %get-tuple-element.57), channel_id=1, source_target_pairs={{0,32},{32,64},{64,96},{96,128},{128,160},{160,192},{192,224},{224... | collective-permute-start | bytes 393224 | tf_op jit(solution)/shard_map/while/body/ppermute | solution.py:15
  178.1 10.3 %collective-permute-start = (bf16[256,256]{1,0:T(8,128)(2,1)S(1)}, bf16[256,256]{1,0:T(8,128)(2,1)S(1)}, u32[]{:S(2)}, u32[]{:S(2)}) collective-permute-start(bf16[256,256]{1,0:T(8,128)(2,1)S(1)} %get-tuple-element.57), channel_id=1, source_target_pairs={{0,32},{32,64},{64,96},{96,128},{128,160},{160,192},{192,224},{224... | collective-permute-start | bytes 393224 | tf_op jit(solution)/shard_map/while/body/ppermute | solution.py:15
  188.4 10.5 %collective-permute-start = (bf16[256,256]{1,0:T(8,128)(2,1)S(1)}, bf16[256,256]{1,0:T(8,128)(2,1)S(1)}, u32[]{:S(2)}, u32[]{:S(2)}) collective-permute-start(bf16[256,256]{1,0:T(8,128)(2,1)S(1)} %get-tuple-element.57), channel_id=1, source_target_pairs={{0,32},{32,64},{64,96},{96,128},{128,160},{160,192},{192,224},{224... | collective-permute-start | bytes 393224 | tf_op jit(solution)/shard_map/while/body/ppermute | solution.py:15
Sparse Core Ops, SparseCore 0:
  13.4 143.1 reduce-scatter.1
  160.2 93.5 all-gather.1
where the time goes:
time: 264 us
  waiting for transfers between devices  229 us (87%)
  between operations  14.8 us (6%)
  matrix products  8.02 us (3%)
  starting transfers between devices  7.76 us (3%)
  other arithmetic  2.77 us (1%)
    reduce_scatter x1, waiting for transfers between devices, body(): lax.psum_scatter(lax.dot_general(columns, upstream, (((0,), (0,)), ((), (...  142 us
    all_gather x1, waiting for transfers between devices, body(): lax.all_gather(weights, 'fsdp', axis=1, tiled=True)[0]  54.2 us
    ppermute x4, waiting for transfers between devices, shifted(): return lax.ppermute(value, axis, pairs)  32.3 us
    ppermute x4, starting transfers between devices, shifted(): return lax.ppermute(value, axis, pairs)  7.68 us
  transfers between devices with their start and end apart: 6, of which 6 were waited for; matrix products, arithmetic and copies ran while one was open for 1% of the time, Pallas kernels for 0%

commit v1 on v0

v1 whole, which is shorter than its diff:
```python
import functools

import jax
import jax.numpy as jnp
from jax import lax
from jax.experimental import pallas as pl
from jax.experimental.pallas import tpu as pltpu
from jax.sharding import PartitionSpec as P

MESH = pl.DeviceIdType.MESH
BF16 = jnp.bfloat16
F32 = jnp.float32
beta_one = 0.9
beta_two = 0.95
learn_rate = 0.001
epsilon = 1e-08
NZ, NY, NC = 4, 4, 2
ORDER = (2, 1, 3, 0)
VMEM_BYTES = 48 * 1024 * 1024


def power_of(base, exponent):
    result = jnp.float32(1.0)
    for bit in range(5):
        factor = jnp.float32(base ** (1 << bit))
        result = result * jnp.where((exponent >> bit) & 1 == 1, factor, jnp.float32(1.0))
    return result


def kernel(
    distance, groups,
    step_ref, act_hbm, cot_hbm, w_hbm, m_hbm, v_hbm,
    kv_out, nw_out, nf_out, ns_out,
    act, cot, cot_t, wts, part, from_core, y_in, z_in, mom1, mom2, own_w, total, kv, local, peer, mixed,
    load_sem, send_sem, recv_sem, store_sem,
):
    group, index = lax.axis_index("gossip"), lax.axis_index("fsdp")
    zi, yi, ci = index // (NY * NC), (index // NC) % NY, index % NC
    rows = w_hbm.shape[1]
    cols = w_hbm.shape[2]
    half = cols // 2

    def place(zr, yr, cr):
        return ((zi + zr) % NZ) * (NY * NC) + ((yi + yr) % NY) * NC + (ci + cr) % NC

    up_z, down_z = (group, place(1, 0, 0)), (group, place(3, 0, 0))
    up_y, down_y = (group, place(0, 1, 0)), (group, place(0, 3, 0))
    other = (group, place(0, 0, 1))
    to_peer = ((group + distance) % groups, index)
    of_peer = ((group + groups - distance) % groups, index)

    barrier = pltpu.get_barrier_semaphore()
    for device in (up_z, down_z, up_y, down_y, other, to_peer, of_peer):
        pl.semaphore_signal(barrier, inc=1, device_id=device, device_id_type=MESH)

    loads = {}

    def load(name, source, target):
        loads[name] = pltpu.make_async_copy(source, target, load_sem.at[len(loads)])
        loads[name].start()

    span = rows * NY * NC
    load("w", w_hbm.at[0], wts.at[0, 0, 0])
    load("cot", cot_hbm.at[0], cot)
    for zr in ORDER:
        window = pl.ds(pl.multiple_of(((zi + zr) % NZ) * span, span), span)
        load(("act", zr), act_hbm.at[0, :, window], act.at[:, window])
    load("m", m_hbm.at[0], mom1)
    load("v", v_hbm.at[0], mom2)
    load("own_w", w_hbm.at[0], own_w)

    copies = {}

    def send(name, source, target, device):
        number = len(copies)
        copies[name] = pltpu.make_async_remote_copy(
            src_ref=source,
            dst_ref=target,
            send_sem=send_sem.at[number],
            recv_sem=recv_sem.at[number],
            device_id=device,
            device_id_type=MESH,
        )
        copies[name].start()

    def arrived(name):
        copies[name].wait_recv()

    top, low = pl.ds(0, rows // 2), pl.ds(rows // 2, rows // 2)

    def gather_core(zr, yr):
        send(("gc", zr, yr), wts.at[0, zr, yr], wts.at[1, zr, yr], other)

    def gather_y(zr):
        send(("gy+", zr), wts.at[0, zr, 0], wts.at[0, zr, 3], up_y)
        send(("gy-", zr), wts.at[0, zr, 0], wts.at[0, zr, 1], down_y)
        gather_core(zr, 0)

    def gather_y_pass(zr):
        arrived(("gy+", zr))
        send(("gyp+", zr), wts.at[0, zr, 3, top], wts.at[0, zr, 2, top], up_y)
        gather_core(zr, 3)
        arrived(("gy-", zr))
        send(("gyp-", zr), wts.at[0, zr, 1, low], wts.at[0, zr, 2, low], down_y)
        gather_core(zr, 1)

    def gather_y_last(zr):
        arrived(("gyp+", zr))
        arrived(("gyp-", zr))
        gather_core(zr, 2)

    def gradient(cr, zr):
        def one(yr, carry):
            window = pl.ds(pl.multiple_of(place(zr, yr, cr) * rows, rows), rows)
            block = jnp.dot(cot_t[...], act[:, window], preferred_element_type=F32)
            part[cr, zr, yr] = block.astype(BF16)
            return carry

        lax.fori_loop(0, NY, one, 0)

    def gradient_other(zr):
        loads[("act", zr)].wait()
        gradient(1, zr)
        send(("rc", zr), part.at[1, zr], from_core.at[zr], other)

    first, second = pl.ds(0, half), pl.ds(half, half)

    def scatter_y(zr):
        arrived(("rc", zr))

        def add(yr):
            part[0, zr, yr] = part[0, zr, yr] + from_core[zr, yr]

        add(2)
        send(("y1a", zr), part.at[0, zr, 2, first], y_in.at[zr, 0], up_y)
        send(("y1b", zr), part.at[0, zr, 2, second], y_in.at[zr, 1], down_y)
        add(1)
        send(("y2b", zr), part.at[0, zr, 1, second], y_in.at[zr, 2], up_y)
        add(3)
        send(("y2a", zr), part.at[0, zr, 3, first], y_in.at[zr, 3], down_y)
        add(0)

    def scatter_y_pass(zr):
        arrived(("y1a", zr))
        part[0, zr, 1, first] = part[0, zr, 1, first] + y_in[zr, 0]
        send(("y3a", zr), part.at[0, zr, 1, first], y_in.at[zr, 4], up_y)
        arrived(("y1b", zr))
        part[0, zr, 3, second] = part[0, zr, 3, second] + y_in[zr, 1]
        send(("y3b", zr), part.at[0, zr, 3, second], y_in.at[zr, 5], down_y)

    def add_three(a, b, c):
        return a.astype(F32) + b.astype(F32) + c.astype(F32)

    def scatter_y_last(zr):
        arrived(("y2a", zr))
        arrived(("y3a", zr))
        part[0, zr, 0, first] = add_three(part[0, zr, 0, first], y_in[zr, 3], y_in[zr, 4]).astype(BF16)
        arrived(("y2b", zr))
        arrived(("y3b", zr))
        part[0, zr, 0, second] = add_three(part[0, zr, 0, second], y_in[zr, 2], y_in[zr, 5]).astype(BF16)

    def forward(cr, zr):
        def one(yr, carry):
            window = pl.ds(pl.multiple_of(place(zr, yr, cr) * rows, rows), rows)
            total[...] += jnp.dot(act[:, window], wts[cr, zr, yr], preferred_element_type=F32)
            return carry

        lax.fori_loop(0, NY, one, 0)

    def forward_other(zr):
        for yr in range(NY):
            arrived(("gc", zr, yr))
        forward(1, zr)

    loads["w"].wait()
    pl.semaphore_wait(barrier, 7)
    mine = wts.at[0, 0, 0]
    send("gz+a", mine.at[top], wts.at[0, 3, 0, top], up_z)
    send("gz-b", mine.at[low], wts.at[0, 1, 0, low], down_z)
    send("gz+b", mine.at[low], wts.at[0, 3, 0, low], up_z)
    send("gz-a", mine.at[top], wts.at[0, 1, 0, top], down_z)
    gather_y(0)
    loads["cot"].wait()
    cot_t[...] = cot[...].T

    gradient_other(2)
    gradient(0, 2)
    gradient_other(1)
    scatter_y(2)
    gradient(0, 1)
    gradient_other(3)
    scatter_y(1)
    gradient(0, 3)
    gradient_other(0)
    scatter_y(3)
    gradient(0, 0)
    scatter_y_pass(2)
    scatter_y(0)
    total[...] = jnp.zeros_like(total)
    gather_y_pass(0)
    scatter_y_pass(1)

    arrived("gz+a")
    send("gzp+", wts.at[0, 3, 0, top], wts.at[0, 2, 0, top], up_z)
    arrived("gz-b")
    send("gzp-", wts.at[0, 1, 0, low], wts.at[0, 2, 0, low], down_z)

    def r(zr, window):
        return part.at[0, zr, 0, window]

    scatter_y_last(2)
    send("z1a", r(2, first), z_in.at[0], up_z)
    send("z1b", r(2, second), z_in.at[1], down_z)
    scatter_y_pass(3)
    scatter_y_last(1)
    send("z2b", r(1, second), z_in.at[2], up_z)
    gather_y_last(0)
    arrived("gz+b")
    gather_y(3)
    arrived("gz-a")
    gather_y(1)
    scatter_y_pass(0)
    scatter_y_last(3)
    send("z2a", r(3, first), z_in.at[3], down_z)
    forward(0, 0)
    forward_other(0)
    arrived("z1a")
    part[0, 1, 0, first] = part[0, 1, 0, first] + z_in[0]
    send("z3a", r(1, first), z_in.at[4], up_z)
    arrived("z1b")
    part[0, 3, 0, second] = part[0, 3, 0, second] + z_in[1]
    send("z3b", r(3, second), z_in.at[5], down_z)
    scatter_y_last(0)
    arrived("gzp+")
    arrived("gzp-")
    gather_y(2)
    gather_y_pass(3)
    gather_y_pass(1)
    gather_y_last(3)
    forward(0, 3)
    gather_y_last(1)
    forward(0, 1)
    forward_other(3)
    forward_other(1)
    gather_y_pass(2)

    loads["m"].wait()
    loads["v"].wait()
    loads["own_w"].wait()
    count = step_ref[0] + 1
    ones = jnp.ones((1, half), F32)
    scale_one = learn_rate / (ones * (1.0 - power_of(beta_one, count)))
    scale_two = 1.0 / (ones * (1.0 - power_of(beta_two, count)))
    stores = []

    def store(source, target):
        copy = pltpu.make_async_copy(source, target, store_sem.at[len(stores)])
        copy.start()
        stores.append(copy)

    def adam(side, window, pure, summed):
        gradient_t = add_three(part[0, 0, 0, window], z_in[pure], z_in[summed])
        grad = gradient_t.T
        next_one = beta_one * mom1[:, window] + (1.0 - beta_one) * grad
        next_two = beta_two * mom2[:, window] + (1.0 - beta_two) * grad * grad
        mom1[:, window] = next_one
        mom2[:, window] = next_two
        update = next_one * scale_one / (jnp.sqrt(next_two * scale_two) + epsilon)
        local[side] = (own_w[:, window].astype(F32) - update).astype(BF16)
        send(("gossip", side), local.at[side], peer.at[side], to_peer)

    arrived("z2a")
    arrived("z3a")
    adam(0, first, 3, 4)
    arrived("z2b")
    arrived("z3b")
    adam(1, second, 2, 5)
    store(mom1, nf_out.at[0])
    store(mom2, ns_out.at[0])

    gather_y_last(2)
    forward(0, 2)
    forward_other(2)
    kv[...] = total[...].astype(BF16)
    store(kv, kv_out.at[0])
    for side, window in ((0, first), (1, second)):
        arrived(("gossip", side))
        average = (local[side].astype(F32) + peer[side].astype(F32)) * 0.5
        mixed[:, window] = average.astype(BF16)
    store(mixed, nw_out.at[0])
    for copy in copies.values():
        copy.wait_send()
    for copy in stores:
        copy.wait()


N_COPIES = 6 + 4 * 4 + 16 + 4 + 6 * 4 + 6 + 2


def solution(mesh):
    groups = mesh.shape["gossip"]

    def body(activations, cotangent, weights, first_moment, second_moment, step_number):
        tokens, width = activations.shape[1:]
        rows, cols = weights.shape[1:]

        def call(distance, number):
            def run(step, *arrays):
                return pl.pallas_call(
                    functools.partial(kernel, distance, groups),
                    out_shape=(
                        jax.ShapeDtypeStruct((1, tokens, cols), BF16),
                        jax.ShapeDtypeStruct((1, rows, cols), BF16),
                        jax.ShapeDtypeStruct((1, rows, cols), F32),
                        jax.ShapeDtypeStruct((1, rows, cols), F32),
                    ),
                    in_specs=[pl.BlockSpec(memory_space=pltpu.SMEM)] + [pl.BlockSpec(memory_space=pl.ANY)] * 5,
                    out_specs=(pl.BlockSpec(memory_space=pl.ANY),) * 4,
                    scratch_shapes=[
                        pltpu.VMEM((tokens, width), BF16),
                        pltpu.VMEM((tokens, cols), BF16),
                        pltpu.VMEM((cols, tokens), BF16),
                        pltpu.VMEM((NC, NZ, NY, rows, cols), BF16),
                        pltpu.VMEM((NC, NZ, NY, cols, rows), BF16),
                        pltpu.VMEM((NZ, NY, cols, rows), BF16),
                        pltpu.VMEM((NZ, 6, cols // 2, rows), BF16),
                        pltpu.VMEM((6, cols // 2, rows), BF16),
                        pltpu.VMEM((rows, cols), F32),
                        pltpu.VMEM((rows, cols), F32),
                        pltpu.VMEM((rows, cols), BF16),
                        pltpu.VMEM((tokens, cols), F32),
                        pltpu.VMEM((tokens, cols), BF16),
                        pltpu.VMEM((2, rows, cols // 2), BF16),
                        pltpu.VMEM((2, rows, cols // 2), BF16),
                        pltpu.VMEM((rows, cols), BF16),
                        pltpu.SemaphoreType.DMA((9,)),
                        pltpu.SemaphoreType.DMA((N_COPIES,)),
                        pltpu.SemaphoreType.DMA((N_COPIES,)),
                        pltpu.SemaphoreType.DMA((4,)),
                    ],
                    compiler_params=pltpu.CompilerParams(
                        collective_id=number, has_side_effects=True, vmem_limit_bytes=VMEM_BYTES
                    ),
                )(step, *arrays)

            return run

        branches = [call(1 << hop, hop) for hop in range(3)]
        return lax.switch(
            step_number[0] % 3, branches,
            step_number, activations, cotangent, weights, first_moment, second_moment,
        )

    spread = P("gossip", "fsdp", None)
    return jax.shard_map(
        body,
        mesh=mesh,
        in_specs=(spread,) * 5 + (P(),),
        out_specs=(spread,) * 4,
        check_vma=False,
    )
```

time: 264 us -> 69.2 us (0.26)
  waiting for transfers between devices: 229 us -> 0 us
  Pallas kernels: 0 us -> 65 us
  between operations: 14.8 us -> 1.3 us
  matrix products: 8.02 us -> 0 us
  starting transfers between devices: 7.76 us -> 0 us
  other arithmetic: 2.77 us -> 0 us
    reduce_scatter x1 -> x0, waiting for transfers between devices: 142 us -> none  [body(): lax.psum_scatter(lax.dot_general(columns, upstream, (((0,), (0,)), ((), (...]
    pallas_call x0 -> x1, Pallas kernels: none -> 65 us  [run(): pl.pallas_call(functools.partial(kernel, distance, groups), out_shape=(ja...]
    all_gather x1 -> x0, waiting for transfers between devices: 54.2 us -> none  [body(): lax.all_gather(weights, 'fsdp', axis=1, tiled=True)[0]]
    ppermute x4 -> x0, waiting for transfers between devices: 32.3 us -> none  [shifted(): return lax.ppermute(value, axis, pairs)]
    dot_general x2 -> x0, matrix products: 8.02 us -> none  [the longest x1 4.21 us: body(): lax.dot_general(columns, upstream, (((0,), (0,)), ((), ())), preferred_el...]
    ppermute x4 -> x0, starting transfers between devices: 7.68 us -> none  [shifted(): return lax.ppermute(value, axis, pairs)]
    broadcast_in_dim x2 -> x0, other arithmetic: 2.77 us -> none  [the longest x1 2.07 us: body(): next_two[None]]
  transfers between devices with their start and end apart: 6 -> 0, of which waited for: 6 -> 0; matrix products, arithmetic and copies ran while one was open for 1% -> 0% of each run, Pallas kernels for 0% -> 0%
where the time goes in v1:
time: 69.2 us; the launch traced here: 69 us
  Pallas kernels  65 us (94%)
  local copies, waits for them, and re-layouts  2.7 us (4%)
  between operations  1.3 us (2%)
    pallas_call x1, Pallas kernels, run(): pl.pallas_call(functools.partial(kernel, distance, groups), out_shape=(ja...  65 us
    unnamed x4, local copies, waits for them, and re-layouts  2.7 us

profile of v1, /device:TPU:1, one launch (start us, length us, event | category | flops | bytes accessed | tf_op | source)
XLA Modules:
  0.0 69.0 jit_solution(11166828330564197499)
XLA Ops:
  1.3 65.0 %conditional.1 = ((bf16[1,192,256]{2,1,0:T(8,128)(2,1)S(1)}, bf16[1,256,256]{2,1,0:T(8,128)(2,1)S(1)}, f32[1,256,256]{2,1,0:T(8,128)S(1)}, f32[1,256,256]{2,1,0:T(8,128)S(1)})) conditional(s32[]{:T(128)} %clamp.3, (s32[1]{0:T(128)}, bf16[1,192,8192]{2,1,0:T(8,128)(2,1)}, bf16[1,192,256]{2,1,0:T(8,128)(2,1)}, ...), branch_computations={%region_0.1_spmd, %region_1.2_spmd, %region_2.3_spmd} | conditional | bytes 8 | solution.py:349
  1.3 65.0 %branch_0_fun.1 = (bf16[1,192,256]{2,1,0:T(8,128)(2,1)S(1)}, bf16[1,256,256]{2,1,0:T(8,128)(2,1)S(1)}, f32[1,256,256]{2,1,0:T(8,128)S(1)}, f32[1,256,256]{2,1,0:T(8,128)S(1)}) custom-call(s32[1]{0:T(128)} %get-tuple-element.36.step_ref, bf16[1,192,8192]{2,1,0:T(8,128)(2,1)} %get-tuple-element.37.act_hbm, bf16[1,192,256]{2,1,0:T(8,128)(2,1)} %get-tuple-element.38.cot_hbm, ...), custom_call_target="tpu_custom_call" | custom-call | tf_op jit(solution)/shard_map/cond/branch_0_fun/pallas_call | solution.py:309
  66.3 0.6 copy.39
  67.0 0.7 copy.40
  67.6 0.7 %copy.41 = f32[1,256,256]{2,1,0:T(8,128)} copy(f32[1,256,256]{2,1,0:T(8,128)S(1)} %get-tuple-element.92) | data formatting | bytes 524288
  68.3 0.7 %copy.42 = f32[1,256,256]{2,1,0:T(8,128)} copy(f32[1,256,256]{2,1,0:T(8,128)S(1)} %get-tuple-element.93) | data formatting | bytes 524288

commit v2 on v1

v2 whole, which is shorter than its diff:
```python
import functools

import jax
import jax.numpy as jnp
from jax import lax
from jax.experimental import pallas as pl
from jax.experimental.pallas import tpu as pltpu
from jax.sharding import PartitionSpec as P

MESH = pl.DeviceIdType.MESH
BF16 = jnp.bfloat16
F32 = jnp.float32
beta_one = 0.9
beta_two = 0.95
learn_rate = 0.001
epsilon = 1e-08
NZ, NY, NC = 4, 4, 2
ORDER = (2, 1, 3, 0)
VMEM_BYTES = 48 * 1024 * 1024


def power_of(base, exponent):
    result = jnp.float32(1.0)
    for bit in range(5):
        factor = jnp.float32(base ** (1 << bit))
        result = result * jnp.where((exponent >> bit) & 1 == 1, factor, jnp.float32(1.0))
    return result


def kernel(
    distance, groups,
    step_ref, act_hbm, cot_hbm, w_hbm, m_hbm, v_hbm,
    kv_out, nw_out, nf_out, ns_out,
    act, cot, cot_t, wts, part, from_core, y_in, z_in, mom1, mom2, own_w, total, kv, local, peer, mixed,
    load_sem, send_sem, recv_sem, store_sem,
):
    group, index = lax.axis_index("gossip"), lax.axis_index("fsdp")
    zi, yi, ci = index // (NY * NC), (index // NC) % NY, index % NC
    rows = w_hbm.shape[1]
    cols = w_hbm.shape[2]
    half = cols // 2

    def place(zr, yr, cr):
        return ((zi + zr) % NZ) * (NY * NC) + ((yi + yr) % NY) * NC + (ci + cr) % NC

    up_z, down_z = (group, place(1, 0, 0)), (group, place(3, 0, 0))
    up_y, down_y = (group, place(0, 1, 0)), (group, place(0, 3, 0))
    other = (group, place(0, 0, 1))
    to_peer = ((group + distance) % groups, index)
    of_peer = ((group + groups - distance) % groups, index)

    barrier = pltpu.get_barrier_semaphore()
    for device in (up_z, down_z, up_y, down_y, other, to_peer, of_peer):
        pl.semaphore_signal(barrier, inc=1, device_id=device, device_id_type=MESH)

    loads = {}

    def load(name, source, target):
        loads[name] = pltpu.make_async_copy(source, target, load_sem.at[len(loads)])
        loads[name].start()

    waited = set()

    def loaded(name):
        if name not in waited:
            waited.add(name)
            loads[name].wait()

    span = rows * NY * NC
    load("w", w_hbm.at[0], wts.at[0, 0, 0])
    load("cot", cot_hbm.at[0], cot)
    for zr in ORDER:
        window = pl.ds(pl.multiple_of(((zi + zr) % NZ) * span, span), span)
        load(("act", zr), act_hbm.at[0, :, window], act.at[:, window])
    load("m", m_hbm.at[0], mom1)
    load("v", v_hbm.at[0], mom2)
    load("own_w", w_hbm.at[0], own_w)

    copies = {}

    def send(name, source, target, device):
        prepare(name, source, target, device)
        copies[name].start()

    def prepare(name, source, target, device):
        number = len(copies)
        copies[name] = pltpu.make_async_remote_copy(
            src_ref=source,
            dst_ref=target,
            send_sem=send_sem.at[number],
            recv_sem=recv_sem.at[number],
            device_id=device,
            device_id_type=MESH,
        )

    seen = set()

    def arrived(name):
        if name in seen:
            return
        seen.add(name)
        copies[name].wait_recv()

    top, low = pl.ds(0, rows // 2), pl.ds(rows // 2, rows // 2)

    def gather_core(zr, yr):
        send(("gc", zr, yr), wts.at[0, zr, yr], wts.at[1, zr, yr], other)

    def gather_y(zr):
        for name in {0: (), 3: ("gz+b",), 1: ("gz-a",), 2: ("gzp+", "gzp-")}[zr]:
            arrived(name)
        send(("gy+", zr), wts.at[0, zr, 0], wts.at[0, zr, 3], up_y)
        send(("gy-", zr), wts.at[0, zr, 0], wts.at[0, zr, 1], down_y)
        gather_core(zr, 0)

    def gather_y_pass_up(zr):
        arrived(("gy+", zr))
        send(("gyp+", zr), wts.at[0, zr, 3, top], wts.at[0, zr, 2, top], up_y)
        gather_core(zr, 3)

    def gather_y_pass_down(zr):
        arrived(("gy-", zr))
        send(("gyp-", zr), wts.at[0, zr, 1, low], wts.at[0, zr, 2, low], down_y)
        gather_core(zr, 1)

    def gather_y_last(zr):
        arrived(("gyp+", zr))
        arrived(("gyp-", zr))
        gather_core(zr, 2)

    def block(zr, yr, cr):
        return pl.ds(pl.multiple_of(place(zr, yr, cr) * rows, rows), rows)

    def gradient(cr, zr):
        loaded(("act", zr))
        for yr in range(NY):
            product = jnp.dot(cot_t[...], act[:, block(zr, yr, cr)], preferred_element_type=F32)
            part[cr, zr, yr] = product.astype(BF16)

    def send_other(zr):
        send(("rc", zr), part.at[1, zr], from_core.at[zr], other)

    first, second = pl.ds(0, half), pl.ds(half, half)

    def add_into(zr, yr, window, other_term):
        part[0, zr, yr, window] = part[0, zr, yr, window] + other_term

    def add_three(a, b, c):
        return a.astype(F32) + b.astype(F32) + c.astype(F32)

    def scatter_y(zr):
        arrived(("rc", zr))
        for yr in (2, 1, 3, 0):
            part[0, zr, yr] = part[0, zr, yr] + from_core[zr, yr]
        send(("y1a", zr), part.at[0, zr, 2, first], y_in.at[zr, 0], up_y)
        send(("y1b", zr), part.at[0, zr, 2, second], y_in.at[zr, 1], down_y)

    def scatter_y_near(zr):
        send(("y2b", zr), part.at[0, zr, 1, second], y_in.at[zr, 2], up_y)
        send(("y2a", zr), part.at[0, zr, 3, first], y_in.at[zr, 3], down_y)

    def scatter_y_pass_a(zr):
        arrived(("y1a", zr))
        add_into(zr, 1, first, y_in[zr, 0])
        send(("y3a", zr), part.at[0, zr, 1, first], y_in.at[zr, 4], up_y)

    def scatter_y_pass_b(zr):
        arrived(("y1b", zr))
        add_into(zr, 3, second, y_in[zr, 1])
        send(("y3b", zr), part.at[0, zr, 3, second], y_in.at[zr, 5], down_y)

    def reduced(zr, window):
        return part.at[0, zr, 0, window]

    def scatter_y_last_a(zr):
        arrived(("y2a", zr))
        arrived(("y3a", zr))
        part[0, zr, 0, first] = add_three(part[0, zr, 0, first], y_in[zr, 3], y_in[zr, 4]).astype(BF16)
        if zr == 2:
            send("z1a", reduced(2, first), z_in.at[0], up_z)
        if zr == 3:
            send("z2a", reduced(3, first), z_in.at[3], down_z)

    def scatter_y_last_b(zr):
        arrived(("y2b", zr))
        arrived(("y3b", zr))
        part[0, zr, 0, second] = add_three(part[0, zr, 0, second], y_in[zr, 2], y_in[zr, 5]).astype(BF16)
        if zr == 2:
            send("z1b", reduced(2, second), z_in.at[1], down_z)
        if zr == 1:
            send("z2b", reduced(1, second), z_in.at[2], up_z)

    pieces = [pl.ds(piece * (rows // PIECES), rows // PIECES) for piece in range(PIECES)]

    def scatter_z_pass_a():
        arrived("z1a")
        add_into(1, 0, first, z_in[0])
        for piece, lanes in enumerate(pieces):
            send(("z3a", piece), part.at[0, 1, 0, first, lanes], z_in.at[4, :, lanes], up_z)

    def scatter_z_pass_b():
        arrived("z1b")
        add_into(3, 0, second, z_in[1])
        for piece, lanes in enumerate(pieces):
            send(("z3b", piece), part.at[0, 3, 0, second, lanes], z_in.at[5, :, lanes], down_z)

    def forward(cr, zr):
        products = [
            jnp.dot(act[:, block(zr, yr, cr)], wts[cr, zr, yr], preferred_element_type=F32) for yr in range(NY)
        ]
        total[...] += (products[0] + products[1]) + (products[2] + products[3])

    def forward_other(zr):
        for yr in range(NY):
            arrived(("gc", zr, yr))
        forward(1, zr)

    def start():
        loaded("w")
        pl.semaphore_wait(barrier, 7)

    lane = group % 4

    def gather_z_one_early():
        mine = wts.at[0, 0, 0]
        prepare("gz+a", mine.at[top], wts.at[0, 3, 0, top], up_z)
        prepare("gz-b", mine.at[low], wts.at[0, 1, 0, low], down_z)

        @pl.when(lane == 0)
        def _():
            copies["gz+a"].start()
            copies["gz-b"].start()

    def gather_z_one_late():
        @pl.when(lane != 0)
        def _():
            copies["gz+a"].start()
            copies["gz-b"].start()

    def gather_z_two():
        mine = wts.at[0, 0, 0]
        send("gz+b", mine.at[low], wts.at[0, 3, 0, low], up_z)
        send("gz-a", mine.at[top], wts.at[0, 1, 0, top], down_z)

    def gather_z_pass_up():
        arrived("gz+a")
        send("gzp+", wts.at[0, 3, 0, top], wts.at[0, 2, 0, top], up_z)

    def gather_z_pass_down():
        arrived("gz-b")
        send("gzp-", wts.at[0, 1, 0, low], wts.at[0, 2, 0, low], down_z)

    def turn():
        loaded("cot")
        cot_t[...] = cot[...].T

    def clear():
        total[...] = jnp.zeros_like(total)

    stores = []

    def store(source, target):
        copy = pltpu.make_async_copy(source, target, store_sem.at[len(stores)])
        copy.start()
        stores.append(copy)

    def adam(side, piece):
        cols_at, lanes = (first, second)[side], pieces[piece]
        pure, summed, name = ((3, 4, "a"), (2, 5, "b"))[side]
        arrived("z2" + name)
        arrived(("z3" + name, piece))
        for name in ("m", "v", "own_w"):
            loaded(name)
        count = step_ref[0] + 1
        ones = jnp.ones((1, half), F32)
        scale_one = learn_rate / (ones * (1.0 - power_of(beta_one, count)))
        scale_two = 1.0 / (ones * (1.0 - power_of(beta_two, count)))
        gradient_t = add_three(part[0, 0, 0, cols_at, lanes], z_in[pure, :, lanes], z_in[summed, :, lanes])
        grad = gradient_t.T
        next_one = beta_one * mom1[lanes, cols_at] + (1.0 - beta_one) * grad
        next_two = beta_two * mom2[lanes, cols_at] + (1.0 - beta_two) * grad * grad
        mom1[lanes, cols_at] = next_one
        mom2[lanes, cols_at] = next_two
        update = next_one * scale_one / (jnp.sqrt(next_two * scale_two) + epsilon)
        local[side, lanes] = (own_w[lanes, cols_at].astype(F32) - update).astype(BF16)
        send(("gossip", side, piece), local.at[side, lanes], peer.at[side, lanes], to_peer)

    def store_moments():
        store(mom1, nf_out.at[0])
        store(mom2, ns_out.at[0])

    def store_kv():
        kv[...] = total[...].astype(BF16)
        store(kv, kv_out.at[0])

    def mix(side, piece):
        cols_at, lanes = (first, second)[side], pieces[piece]
        arrived(("gossip", side, piece))
        average = (local[side, lanes].astype(F32) + peer[side, lanes].astype(F32)) * 0.5
        mixed[lanes, cols_at] = average.astype(BF16)

    def store_mixed(piece):
        store(mixed.at[pieces[piece]], nw_out.at[0, pieces[piece]])

    turn()
    gradient(0, 1)
    gradient(0, 2)
    gradient(1, 2)
    gradient(1, 3)
    start()
    gather_z_one_early()
    gradient(1, 1)
    clear()
    send_other(2)
    send_other(1)
    gather_y(0)
    gather_z_one_late()
    scatter_y(2)
    gradient(1, 0)
    gradient(0, 3)
    send_other(3)
    scatter_y(1)
    gather_z_two()
    scatter_y_near(2)
    scatter_y(3)
    send_other(0)
    scatter_y_pass_a(2)
    scatter_y_pass_b(2)
    gather_z_pass_down()
    gradient(0, 0)
    scatter_y_near(3)
    gather_z_pass_up()
    scatter_y_near(1)
    scatter_y_pass_a(3)
    scatter_y_pass_b(3)
    scatter_y_pass_a(1)
    scatter_y(0)
    scatter_y_last_a(2)
    scatter_y_pass_b(1)
    scatter_y_last_b(2)
    gather_y(1)
    gather_y(3)
    gather_y_pass_down(0)
    scatter_y_last_a(3)
    gather_y(2)
    scatter_y_last_b(1)
    scatter_y_pass_a(0)
    gather_y_pass_up(0)
    scatter_y_last_a(1)
    scatter_y_pass_b(0)
    scatter_z_pass_a()
    scatter_y_last_b(3)
    gather_y_pass_down(3)
    scatter_z_pass_b()
    scatter_y_near(0)
    gather_y_pass_down(2)
    gather_y_pass_up(2)
    gather_y_pass_up(3)
    gather_y_pass_down(1)
    scatter_y_last_a(0)
    gather_y_pass_up(1)
    scatter_y_last_b(0)
    adam(0, 0)
    adam(1, 0)
    gather_y_last(0)
    adam(0, 1)
    adam(1, 1)
    store_moments()
    gather_y_last(2)
    gather_y_last(3)
    forward(0, 2)
    forward(0, 0)
    gather_y_last(1)
    forward(0, 1)
    forward(0, 3)
    forward_other(3)
    forward_other(2)
    mix(1, 0)
    forward_other(0)
    forward_other(1)
    mix(0, 0)
    store_mixed(0)
    store_kv()
    mix(0, 1)
    mix(1, 1)
    store_mixed(1)
    for name in copies:
        if name not in seen:
            arrived(name)
    for name in loads:
        loaded(name)
    for copy in copies.values():
        copy.wait_send()
    for copy in stores:
        copy.wait()


PIECES = 2
def finish_kernel(*refs):
    count = (len(refs) - 1) // 2
    moves = [pltpu.make_async_copy(refs[i], refs[count + i], refs[-1].at[i]) for i in range(count)]
    for move in moves:
        move.start()
    for move in moves:
        move.wait()


def finish(*arrays):
    return pl.pallas_call(
        finish_kernel,
        out_shape=tuple(jax.ShapeDtypeStruct(array.shape, array.dtype) for array in arrays),
        in_specs=[pl.BlockSpec(memory_space=pl.ANY)] * len(arrays),
        out_specs=(pl.BlockSpec(memory_space=pl.ANY),) * len(arrays),
        scratch_shapes=[pltpu.SemaphoreType.DMA((len(arrays),))],
    )(*arrays)


N_COPIES = 6 + 4 * 4 + 16 + 4 + 6 * 4 + 4 + 4 * PIECES


def solution(mesh):
    groups = mesh.shape["gossip"]

    def body(activations, cotangent, weights, first_moment, second_moment, step_number):
        tokens, width = activations.shape[1:]
        rows, cols = weights.shape[1:]

        def call(distance, number):
            def run(step, *arrays):
                return pl.pallas_call(
                    functools.partial(kernel, distance, groups),
                    out_shape=(
                        jax.ShapeDtypeStruct((1, tokens, cols), BF16),
                        jax.ShapeDtypeStruct((1, rows, cols), BF16),
                        jax.ShapeDtypeStruct((1, rows, cols), F32),
                        jax.ShapeDtypeStruct((1, rows, cols), F32),
                    ),
                    in_specs=[pl.BlockSpec(memory_space=pltpu.SMEM)] + [pl.BlockSpec(memory_space=pl.ANY)] * 5,
                    out_specs=(pl.BlockSpec(memory_space=pl.ANY),) * 4,
                    scratch_shapes=[
                        pltpu.VMEM((tokens, width), BF16),
                        pltpu.VMEM((tokens, cols), BF16),
                        pltpu.VMEM((cols, tokens), BF16),
                        pltpu.VMEM((NC, NZ, NY, rows, cols), BF16),
                        pltpu.VMEM((NC, NZ, NY, cols, rows), BF16),
                        pltpu.VMEM((NZ, NY, cols, rows), BF16),
                        pltpu.VMEM((NZ, 6, cols // 2, rows), BF16),
                        pltpu.VMEM((6, cols // 2, rows), BF16),
                        pltpu.VMEM((rows, cols), F32),
                        pltpu.VMEM((rows, cols), F32),
                        pltpu.VMEM((rows, cols), BF16),
                        pltpu.VMEM((tokens, cols), F32),
                        pltpu.VMEM((tokens, cols), BF16),
                        pltpu.VMEM((2, rows, cols // 2), BF16),
                        pltpu.VMEM((2, rows, cols // 2), BF16),
                        pltpu.VMEM((rows, cols), BF16),
                        pltpu.SemaphoreType.DMA((9,)),
                        pltpu.SemaphoreType.DMA((N_COPIES,)),
                        pltpu.SemaphoreType.DMA((N_COPIES,)),
                        pltpu.SemaphoreType.DMA((3 + PIECES,)),
                    ],
                    compiler_params=pltpu.CompilerParams(
                        collective_id=number, has_side_effects=True, vmem_limit_bytes=VMEM_BYTES
                    ),
                )(step, *arrays)

            return run

        branches = [call(1 << hop, hop) for hop in range(3)]
        results = lax.switch(
            step_number[0] % 3, branches,
            step_number, activations, cotangent, weights, first_moment, second_moment,
        )
        return finish(*results)

    spread = P("gossip", "fsdp", None)
    return jax.shard_map(
        body,
        mesh=mesh,
        in_specs=(spread,) * 5 + (P(),),
        out_specs=(spread,) * 4,
        check_vma=False,
    )
```

time: 69.2 us -> 63.5 us (0.918)
  the two profiles are of different devices: /device:TPU:1 before, /device:TPU:16 now
where the time goes in v2:
time: 63.5 us; the launch traced here: 63.4 us
  Pallas kernels  61.6 us (97%)
  between operations  1.48 us (2%)
    pallas_call x1, Pallas kernels, run(): pl.pallas_call(functools.partial(kernel, distance, groups), out_shape=(ja...  60.7 us

profile of v2, /device:TPU:16, one launch (start us, length us, event | category | flops | bytes accessed | tf_op | source)
XLA Modules:
  0.0 63.4 jit_solution(14185784641549445033)
XLA Ops:
  1.3 61.0 %conditional.1 = ((bf16[1,192,256]{2,1,0:T(8,128)(2,1)S(1)}, bf16[1,256,256]{2,1,0:T(8,128)(2,1)S(1)}, f32[1,256,256]{2,1,0:T(8,128)S(1)}, f32[1,256,256]{2,1,0:T(8,128)S(1)})) conditional(s32[]{:T(128)} %clamp.3, (s32[1]{0:T(128)}, bf16[1,192,8192]{2,1,0:T(8,128)(2,1)}, bf16[1,192,256]{2,1,0:T(8,128)(2,1)}, ...), branch_computations={%region_0.1_spmd, %region_1.2_spmd, %region_2.3_spmd} | conditional | bytes 8 | solution.py:470
  1.3 60.7 %branch_0_fun.1 = (bf16[1,192,256]{2,1,0:T(8,128)(2,1)S(1)}, bf16[1,256,256]{2,1,0:T(8,128)(2,1)S(1)}, f32[1,256,256]{2,1,0:T(8,128)S(1)}, f32[1,256,256]{2,1,0:T(8,128)S(1)}) custom-call(s32[1]{0:T(128)} %get-tuple-element.36.step_ref, bf16[1,192,8192]{2,1,0:T(8,128)(2,1)} %get-tuple-element.37.act_hbm, bf16[1,192,256]{2,1,0:T(8,128)(2,1)} %get-tuple-element.38.cot_hbm, ...), custom_call_target="tpu_custom_call" | custom-call | tf_op jit(solution)/shard_map/cond/branch_0_fun/pallas_call | solution.py:430
  62.3 0.9 %shard_map.93 = (bf16[1,192,256]{2,1,0:T(8,128)(2,1)}, bf16[1,256,256]{2,1,0:T(8,128)(2,1)}, f32[1,256,256]{2,1,0:T(8,128)}, f32[1,256,256]{2,1,0:T(8,128)}) custom-call(bf16[1,192,256]{2,1,0:T(8,128)(2,1)S(1)} %get-tuple-element.62.refs_0_, bf16[1,256,256]{2,1,0:T(8,128)(2,1)S(1)} %get-tuple-element.63.refs_1_, ...), custom_call_target="tpu_custom_call" | custom-call | tf_op jit(solution)/shard_map/pallas_call | solution.py:409
